TPU v7x, 32 devices: a whole 2x2x4 slice. The times are simulated.
32 devices in a mesh: gx: 8 (over y, x, core), gy: 4 (over z).
Axes of the slice: x: 2, y: 2, z: 4, core: 2. Of those that a mesh axis runs over, the one named last changes fastest.
Arguments:
- saved_fluid: bfloat16 [3, 19, 8, 64, 512], P(None, None, None, 'gx', 'gy'), may hold values from 0.019897461 to 0.099609375
- saved_tracer: bfloat16 [3, 7, 8, 64, 512], P(None, None, None, 'gx', 'gy'), may hold values from 0.049804688 to 0.25
- adjoint_fluid: float32 [19, 8, 64, 512], P(None, None, 'gx', 'gy'), may hold values from -6 to 6
- adjoint_tracer: float32 [7, 8, 64, 512], P(None, None, 'gx', 'gy'), may hold values from -6 to 6
- label: int32 [8, 64, 512], P(None, 'gx', 'gy'), may hold values from 0 to 2
Outputs:
- fluid_sensitivity: float32 [19, 8, 64, 512], P(None, None, 'gx', 'gy')
- tracer_sensitivity: float32 [7, 8, 64, 512], P(None, None, 'gx', 'gy')
Inputs may be any that keep to these rules, and one draw needn't show every extreme that they name: `label`: 0 marks a fluid voxel, 1 solid rock, 2 a fluid voxel at an adsorbing site.
All inputs are finite; a program needn't handle non-finite values.
Results may differ from a plain program's by a relative error of at most 0.0003.
Values sent between devices are 32-bit elements; how exact they have to be, the bound alone decides.
A program may use at most 64 MiB of HBM per device.

v0:
```python
import jax
import jax.numpy as jnp
import numpy as np
from jax import lax
from jax.sharding import PartitionSpec as P

TRACER_RATE = 1.3
ADSORB = 0.3
NEXT_COLUMNS = [1, 7, 9, 11, 13, 20]
PRIOR_COLUMNS = [2, 8, 10, 12, 14, 21]
NEXT_ROWS = [3, 7, 10, 15, 17, 22]
PRIOR_ROWS = [4, 8, 9, 16, 18, 23]


def from_behind(value, axis, steps):
    count = lax.axis_size(axis)
    pairs = [(source, (source + steps) % count) for source in range(count)]
    return lax.ppermute(value, axis, pairs)


def lattice():
    return np.array(
        [
            [0, 0, 0],
            [1, 0, 0],
            [-1, 0, 0],
            [0, 1, 0],
            [0, -1, 0],
            [0, 0, 1],
            [0, 0, -1],
            [1, 1, 0],
            [-1, -1, 0],
            [1, -1, 0],
            [-1, 1, 0],
            [1, 0, 1],
            [-1, 0, -1],
            [1, 0, -1],
            [-1, 0, 1],
            [0, 1, 1],
            [0, -1, -1],
            [0, 1, -1],
            [0, -1, 1],
        ]
    )


def opposite(count):
    return [0] + [number + 1 if number % 2 == 1 else number - 1 for number in range(1, count)]


def collision_matrix():
    speeds = lattice()
    along_x, along_y, along_z = (speeds[:, 0], speeds[:, 1], speeds[:, 2])
    square = along_x**2 + along_y**2 + along_z**2
    basis = [
        np.ones(19),
        square,
        square**2,
        along_x,
        square * along_x,
        along_y,
        square * along_y,
        along_z,
        square * along_z,
        3 * along_x**2 - square,
        square * (3 * along_x**2 - square),
        along_y**2 - along_z**2,
        square * (along_y**2 - along_z**2),
        along_x * along_y,
        along_y * along_z,
        along_x * along_z,
        along_x * (along_y**2 - along_z**2),
        along_y * (along_z**2 - along_x**2),
        along_z * (along_x**2 - along_y**2),
    ]
    built = []
    for vector in basis:
        for other in built:
            vector = vector - vector @ other / (other @ other) * other
        built.append(vector)
    moments = np.stack(built)
    inverse = moments.T / np.sum(moments**2, axis=1)
    rates = np.array(
        [
            0,
            1.19,
            1.4,
            0,
            1.2,
            0,
            1.2,
            0,
            1.2,
            1.25,
            1.4,
            1.25,
            1.4,
            1.25,
            1.25,
            1.25,
            1.98,
            1.98,
            1.98,
        ]
    )
    return inverse * rates @ moments


def collide(fluid, tracer, label, table):
    speeds = lattice().astype(np.float32)
    extra = (1,) * (fluid.ndim - 1)
    fluid_weights = np.array(
        [1.0 / 3.0] + [1.0 / 18.0] * 6 + [1.0 / 36.0] * 12, np.float32
    ).reshape((19,) + extra)
    tracer_weights = np.array([0.25] + [0.125] * 6, np.float32).reshape((7,) + extra)
    density = jnp.sum(fluid, axis=0)
    velocity = (
        jnp.tensordot(jnp.asarray(speeds.T), fluid, axes=1, precision=lax.Precision.HIGHEST)
        / density
    )
    projection = jnp.tensordot(
        jnp.asarray(speeds), velocity, axes=1, precision=lax.Precision.HIGHEST
    )
    speed_square = jnp.sum(velocity * velocity, axis=0)
    equilibrium = (
        fluid_weights
        * density
        * (1.0 + 3.0 * projection + 4.5 * projection * projection - 1.5 * speed_square)
    )
    relaxed = fluid - jnp.tensordot(
        table, fluid - equilibrium, axes=1, precision=lax.Precision.HIGHEST
    )
    solid = label == 1
    fluid_out = jnp.where(solid, jnp.stack([fluid[other] for other in opposite(19)]), relaxed)
    amount = jnp.sum(tracer, axis=0)
    tracer_eq = tracer_weights * amount * (1.0 + 4.0 * projection[:7])
    kept = jnp.where(label == 2, 1.0 - ADSORB, 1.0)
    tracer_relaxed = (tracer - TRACER_RATE * (tracer - tracer_eq)) * kept
    tracer_out = jnp.where(
        solid, jnp.stack([tracer[other] for other in opposite(7)]), tracer_relaxed
    )
    return (fluid_out, tracer_out)


def pull_leaving(combined, speeds):
    from_next = from_behind(
        jnp.stack([combined[number, :, 0, :] for number in NEXT_COLUMNS]), "gx", -1
    )
    from_prior = from_behind(
        jnp.stack([combined[number, :, -1, :] for number in PRIOR_COLUMNS]), "gx", 1
    )
    moved = []
    for number in range(combined.shape[0]):
        field = combined[number]
        step_x = speeds[number][0]
        if step_x == 1:
            field = jnp.concatenate(
                [field[:, 1:, :], from_next[NEXT_COLUMNS.index(number)][:, None, :]], axis=1
            )
        elif step_x == -1:
            field = jnp.concatenate(
                [from_prior[PRIOR_COLUMNS.index(number)][:, None, :], field[:, :-1, :]], axis=1
            )
        moved.append(field)
    from_above = from_behind(jnp.stack([moved[number][:, :, 0] for number in NEXT_ROWS]), "gy", -1)
    from_below = from_behind(jnp.stack([moved[number][:, :, -1] for number in PRIOR_ROWS]), "gy", 1)
    pieces = []
    for number in range(combined.shape[0]):
        field = moved[number]
        step_y = speeds[number][1]
        if step_y == 1:
            field = jnp.concatenate(
                [field[:, :, 1:], from_above[NEXT_ROWS.index(number)][:, :, None]], axis=2
            )
        elif step_y == -1:
            field = jnp.concatenate(
                [from_below[PRIOR_ROWS.index(number)][:, :, None], field[:, :, :-1]], axis=2
            )
        pieces.append(jnp.roll(field, -speeds[number][2], axis=0))
    return jnp.stack(pieces)


def body(saved_fluid, saved_tracer, adjoint_fluid, adjoint_tracer, label):
    table = jnp.asarray(collision_matrix(), jnp.float32)
    speeds = [tuple((int(value) for value in row)) for row in lattice()]
    speeds = speeds + speeds[:7]

    def plane_adjoint(operands):
        fluid, tracer, plane_label, pulled_fluid, pulled_tracer = operands
        _, pullback = jax.vjp(
            lambda first, second: collide(first, second, plane_label, table), fluid, tracer
        )
        return pullback((pulled_fluid, pulled_tracer))

    for step in reversed(range(saved_fluid.shape[0])):
        combined = jnp.concatenate([adjoint_fluid, adjoint_tracer], axis=0)
        pulled = pull_leaving(combined, speeds)
        operands = (
            jnp.swapaxes(saved_fluid[step].astype(jnp.float32), 0, 1),
            jnp.swapaxes(saved_tracer[step].astype(jnp.float32), 0, 1),
            label,
            jnp.swapaxes(pulled[:19], 0, 1),
            jnp.swapaxes(pulled[19:], 0, 1),
        )
        new_fluid, new_tracer = lax.map(plane_adjoint, operands)
        adjoint_fluid = jnp.swapaxes(new_fluid, 0, 1)
        adjoint_tracer = jnp.swapaxes(new_tracer, 0, 1)
    return (adjoint_fluid, adjoint_tracer)


def solution(mesh):
    placed = (
        P(None, None, None, "gx", "gy"),
        P(None, None, None, "gx", "gy"),
        P(None, None, "gx", "gy"),
        P(None, None, "gx", "gy"),
        P(None, "gx", "gy"),
    )
    return jax.shard_map(
        body,
        mesh=mesh,
        in_specs=placed,
        out_specs=(P(None, None, "gx", "gy"), P(None, None, "gx", "gy")),
        check_vma=False,
    )
```

profile of v0, /device:TPU:0, one launch (start us, length us, event | category | flops | bytes accessed | tf_op | source)
XLA Modules:
  0.0 232.8 jit_solution(9334405428443547806)
XLA Ops:
  5.9 3.3 %collective-permute-start = (f32[6,8,128]{2,1,0:T(8,128)}, f32[6,8,128]{2,1,0:T(8,128)}, u32[]{:S(2)}, u32[]{:S(2)}) collective-permute-start(f32[6,8,128]{2,1,0:T(8,128)} %constant_dynamic-update-slice_fusion), channel_id=1, source_target_pairs={{0,28},{4,0},{8,4},{12,8},{16,12},{20,16},{24,20},{28,24},{1,29},{... | collective-permute-start | bytes 73736 | tf_op jit(solution)/shard_map/ppermute | solution.py:18
  12.8 1.7 slice_bitcast_fusion.50
  15.2 1.4 slice_bitcast_fusion.58
  16.6 1.3 slice_bitcast_fusion.166
  20.3 1.1 convert_bitcast_fusion.2
  21.4 1.6 convert_bitcast_fusion
  26.0 1.0 copy.1661
  27.0 1.0 copy.1662
  28.0 1.0 copy.1663
  31.1 1.0 copy.1667
  32.6 1.8 copy.1527
  35.8 1.9 slice.1652
  37.7 1.2 copy.1540
  38.9 1.9 slice.1657
  40.8 1.8 copy.1543
  42.6 1.9 slice.1658
  44.5 1.8 copy.1544
  47.1 1.3 copy.1547
  49.9 1.8 copy.1552
  51.9 1.3 fusion.243
  53.5 1.0 pad_maximum_fusion.3
  55.2 1.3 fusion.242
  57.6 1.3 constant_dynamic-update-slice_fusion.14
  58.9 1.3 constant_dynamic-update-slice_fusion.13
  60.2 1.2 constant_dynamic-update-slice_fusion.12
  61.4 3.6 %collective-permute-start.2 = (f32[6,8,8]{2,1,0:T(8,128)}, f32[6,8,8]{2,1,0:T(8,128)}, u32[]{:S(2)}, u32[]{:S(2)}) collective-permute-start(f32[6,8,8]{2,1,0:T(8,128)} %constant_dynamic-update-slice_fusion.12), channel_id=1, source_target_pairs={{0,3},{1,0},{2,1},{3,2},{4,7},{5,4},{6,5},{7,6},{8,11},{9,8},{10,9... | collective-permute-start | bytes 4616 | tf_op jit(solution)/shard_map/ppermute | solution.py:18
  66.4 1.0 pad_maximum_fusion.1
  68.1 1.3 constant_dynamic-update-slice_fusion.20
  69.5 1.3 constant_dynamic-update-slice_fusion.19
  88.1 31.1 %while.39 = (s32[]{:T(128)}, f32[8,19,8,128]{3,1,2,0:T(8,128)S(1)}, f32[8,7,8,128]{3,0,2,1:T(8,128)S(1)}, s32[8,8,128]{2,1,0:T(8,128)S(1)}, f32[8,19,8,128]{3,2,...) while((s32[]{:T(128)}, f32[8,19,8,128]{3,1,2,0:T(8,128)S(1)}, ...), condition=%wide.region_8.9_spmd.clone, body=%wide.region_0.8_spmd.sunk.clone.sunk | while | flops 8554504 | bytes 2164161 | solution.py:205
  89.1 1.1 multiply_reduce_fusion.12
  92.9 1.1 multiply_reduce_fusion.12
  96.8 1.1 multiply_reduce_fusion.12
  100.7 1.1 multiply_reduce_fusion.12
  104.6 1.1 multiply_reduce_fusion.12
  108.5 1.1 multiply_reduce_fusion.12
  112.3 1.1 multiply_reduce_fusion.12
  116.2 1.1 multiply_reduce_fusion.12
  119.8 1.6 collective-permute-start.4
  123.2 2.3 collective-permute-done.5
  126.0 3.6 %collective-permute-start.6 = (f32[6,8,8]{2,1,0:T(8,128)S(1)}, f32[6,8,8]{2,1,0:T(8,128)S(1)}, u32[]{:S(2)}, u32[]{:S(2)}) collective-permute-start(f32[6,8,8]{2,1,0:T(8,128)S(1)} %constant_dynamic-update-slice_fusion.62), channel_id=1, source_target_pairs={{0,3},{1,0},{2,1},{3,2},{4,7},{5,4},{6,5},{7,6},{8,11},{9,8},{10,9... | collective-permute-start | bytes 4616 | tf_op jit(solution)/shard_map/ppermute | solution.py:18
  131.2 4.5 %collective-permute-done.7 = f32[6,8,8]{2,1,0:T(8,128)S(1)} collective-permute-done((f32[6,8,8]{2,1,0:T(8,128)S(1)}, f32[6,8,8]{2,1,0:T(8,128)S(1)}, u32[]{:S(2)}, u32[]{:S(2)}) %collective-permute-start.7) | collective-permute-done | bytes 1568 | tf_op jit(solution)/shard_map/ppermute | solution.py:18
  138.5 37.4 %while.40 = (s32[]{:T(128)}, f32[8,19,8,128]{3,1,2,0:T(8,128)S(1)}, f32[8,7,8,128]{3,0,2,1:T(8,128)S(1)}, s32[8,8,128]{2,1,0:T(8,128)S(1)}, f32[8,19,8,128]{3,0,...) while((s32[]{:T(128)}, f32[8,19,8,128]{3,1,2,0:T(8,128)S(1)}, ...), condition=%wide.region_17.18_spmd.clone, body=%wide.region_9.17_spmd.sunk.clone.sunk | while | flops 8554504 | bytes 2164161 | solution.py:205
  139.5 1.1 multiply_reduce_fusion.14
  144.1 1.1 multiply_reduce_fusion.14
  148.8 1.1 multiply_reduce_fusion.14
  153.5 1.1 multiply_reduce_fusion.14
  158.2 1.1 multiply_reduce_fusion.14
  162.8 1.1 multiply_reduce_fusion.14
  167.5 1.1 multiply_reduce_fusion.14
  172.2 1.1 multiply_reduce_fusion.14
  177.0 2.6 %collective-permute-start.8 = (f32[6,8,128]{2,1,0:T(8,128)S(1)}, f32[6,8,128]{2,1,0:T(8,128)S(1)}, u32[]{:S(2)}, u32[]{:S(2)}) collective-permute-start(f32[6,8,128]{2,1,0:T(8,128)S(1)} %get-tuple-element.867), channel_id=1, source_target_pairs={{0,28},{4,0},{8,4},{12,8},{16,12},{20,16},{24,20},{28,24},{1,29},{... | collective-permute-start | bytes 73736 | tf_op jit(solution)/shard_map/ppermute | solution.py:18
  181.9 2.1 collective-permute-start.11
  184.0 1.2 collective-permute-done.10
  185.4 2.2 collective-permute-done.11
  190.9 41.2 %while.41 = (s32[]{:T(128)}, f32[8,19,8,128]{3,2,0,1:T(8,128)}, f32[8,7,8,128]{3,2,0,1:T(8,128)S(1)}, s32[8,8,128]{2,1,0:T(8,128)S(1)}, f32[8,19,8,128]{3,0,2,1:...) while((s32[]{:T(128)}, f32[8,19,8,128]{3,2,0,1:T(8,128)}, ...), condition=%wide.region_26.27_spmd.clone, body=%wide.region_18.26_spmd.sunk.clone.sunk | while | flops 8554504 | bytes 2219692 | solution.py:205
  191.9 1.1 multiply_reduce_fusion.16
  197.0 1.1 multiply_reduce_fusion.16
  202.2 1.1 multiply_reduce_fusion.16
  207.3 1.1 multiply_reduce_fusion.16
  212.5 1.1 multiply_reduce_fusion.16
  217.6 1.1 multiply_reduce_fusion.16
  222.8 1.1 multiply_reduce_fusion.16
  227.9 1.1 multiply_reduce_fusion.16
  (898 shorter events, 137.1 us)
Async XLA Ops:
  5.9 46.0 %collective-permute-start = (f32[6,8,128]{2,1,0:T(8,128)}, f32[6,8,128]{2,1,0:T(8,128)}, u32[]{:S(2)}, u32[]{:S(2)}) collective-permute-start(f32[6,8,128]{2,1,0:T(8,128)} %constant_dynamic-update-slice_fusion), channel_id=1, source_target_pairs={{0,28},{4,0},{8,4},{12,8},{16,12},{20,16},{24,20},{28,24},{1,29},{... | collective-permute-start | bytes 73736 | tf_op jit(solution)/shard_map/ppermute | solution.py:18
  12.8 1.8 copy-start.9
  12.8 42.4 %collective-permute-start.1 = (f32[6,8,128]{2,1,0:T(8,128)}, f32[6,8,128]{2,1,0:T(8,128)}, u32[]{:S(2)}, u32[]{:S(2)}) collective-permute-start(f32[6,8,128]{2,1,0:T(8,128)} %constant_dynamic-update-slice_fusion.6), channel_id=1, source_target_pairs={{0,4},{4,8},{8,12},{12,16},{16,20},{20,24},{24,28},{28,0},{1,5},{5... | collective-permute-start | bytes 73736 | tf_op jit(solution)/shard_map/ppermute | solution.py:18
  14.5 5.7 %copy-start.4 = (bf16[3,19,8,8,128]{4,3,2,1,0:T(8,128)(2,1)S(1)}, bf16[3,19,8,8,128]{4,3,2,1,0:T(8,128)(2,1)}, u32[]{:S(2)}) copy-start(bf16[3,19,8,8,128]{4,3,2,1,0:T(8,128)(2,1)} %param.24) | copy-start | bytes 2801668
  20.3 1.1 copy-start.7
  32.3 14.0 %copy-start = (f32[1,8,8,128]{2,1,3,0:T(8,128)}, f32[1,8,8,128]{2,1,3,0:T(8,128)S(1)}, u32[]{:S(2)}) copy-start(f32[1,8,8,128]{2,1,3,0:T(8,128)S(1)} %copy.1668) | copy-start | bytes 98308
  32.6 1.8 copy-start.20
  34.4 0.8 copy-start.19
  47.1 1.9 copy-start.1
  61.4 14.1 %collective-permute-start.2 = (f32[6,8,8]{2,1,0:T(8,128)}, f32[6,8,8]{2,1,0:T(8,128)}, u32[]{:S(2)}, u32[]{:S(2)}) collective-permute-start(f32[6,8,8]{2,1,0:T(8,128)} %constant_dynamic-update-slice_fusion.12), channel_id=1, source_target_pairs={{0,3},{1,0},{2,1},{3,2},{4,7},{5,4},{6,5},{7,6},{8,11},{9,8},{10,9... | collective-permute-start | bytes 4616 | tf_op jit(solution)/shard_map/ppermute | solution.py:18
  67.5 3.9 %copy-start.22 = (f32[8,7,128]{2,1,0:T(8,128)S(1)}, f32[8,7,128]{2,1,0:T(8,128)}, u32[]{:S(2)}) copy-start(f32[8,7,128]{2,1,0:T(8,128)} %slice.1612) | copy-start | bytes 86020
  67.5 3.9 %copy-start.31 = (f32[1,8,128]{2,1,0:T(8,128)S(1)}, f32[1,8,128]{2,1,0:T(8,128)}, u32[]{:S(2)}) copy-start(f32[1,8,128]{2,1,0:T(8,128)} %get-tuple-element.961) | copy-start | bytes 12292
  67.5 4.5 %copy-start.17 = (f32[8,8,128]{2,1,0:T(8,128)S(1)}, f32[8,8,128]{2,1,0:T(8,128)}, u32[]{:S(2)}) copy-start(f32[8,8,128]{2,1,0:T(8,128)} %get-tuple-element.832) | copy-start | bytes 98308
  67.5 4.5 %copy-start.33 = (f32[1,8,128]{2,1,0:T(8,128)S(1)}, f32[1,8,128]{2,1,0:T(8,128)}, u32[]{:S(2)}) copy-start(f32[1,8,128]{2,1,0:T(8,128)} %get-tuple-element.955) | copy-start | bytes 12292
  67.5 5.1 %copy-start.23 = (f32[8,7,128]{2,1,0:T(8,128)S(1)}, f32[8,7,128]{2,1,0:T(8,128)}, u32[]{:S(2)}) copy-start(f32[8,7,128]{2,1,0:T(8,128)} %slice.1664) | copy-start | bytes 86020
  67.5 6.6 %copy-start.2 = (f32[8,8,127]{1,0,2:T(8,128)S(1)}, f32[8,8,127]{1,0,2:T(8,128)}, u32[]{:S(2)}) copy-start(f32[8,8,127]{1,0,2:T(8,128)} %pad_maximum_fusion.3) | copy-start | bytes 97540
  68.1 4.4 %copy-start.10 = (f32[7,8,8,128]{3,2,1,0:T(8,128)S(1)}, f32[7,8,8,128]{3,2,1,0:T(8,128)}, u32[]{:S(2)}) copy-start(f32[7,8,8,128]{3,2,1,0:T(8,128)} %get-tuple-element.885) | copy-start | bytes 688132
  71.3 5.8 %collective-permute-start.3 = (f32[6,8,8]{2,1,0:T(8,128)}, f32[6,8,8]{2,1,0:T(8,128)S(1)}, u32[]{:S(2)}, u32[]{:S(2)}) collective-permute-start(f32[6,8,8]{2,1,0:T(8,128)} %constant_dynamic-update-slice_fusion.18), channel_id=1, source_target_pairs={{0,1},{1,2},{2,3},{3,0},{4,5},{5,6},{6,7},{7,4},{8,9},{9,10},{10,1... | collective-permute-start | bytes 4616 | tf_op jit(solution)/shard_map/ppermute | solution.py:18
  72.6 0.7 copy-start.30
  73.3 0.8 copy-start.18
  73.3 0.7 copy-start.32
  74.1 1.0 copy-start.3
  75.3 3.2 %copy-start.8 = (f32[19,8,8,128]{3,2,1,0:T(8,128)S(1)}, f32[19,8,8,128]{3,2,1,0:T(8,128)}, u32[]{:S(2)}) copy-start(f32[19,8,8,128]{3,2,1,0:T(8,128)} %constant_dynamic-update-slice_fusion.40) | copy-start | bytes 1867780
  78.3 0.8 copy-start.14
  79.0 0.8 copy-start.15
  79.8 0.7 copy-start.28
  79.8 0.7 copy-start.37
  80.5 0.7 copy-start.27
  80.5 0.7 copy-start.36
  81.6 0.8 copy-start.16
  81.6 0.7 copy-start.29
  82.4 0.8 copy-start.21
  83.3 0.8 copy-start.13
  84.1 0.8 copy-start.12
  84.9 0.8 copy-start.11
  85.8 0.8 copy-start.26
  85.8 0.8 copy-start.35
  86.5 0.7 copy-start.25
  86.5 0.7 copy-start.34
  87.3 0.7 copy-start.5
  87.3 0.8 copy-start.6
  87.3 0.8 copy-start.24
  87.4 0.7 copy-start.40
  87.4 0.7 copy-start.41
  87.4 0.7 copy-start.42
  87.4 0.7 copy-start.43
  87.4 0.7 copy-start.44
  119.8 6.0 %collective-permute-start.4 = (f32[6,8,128]{2,1,0:T(8,128)S(1)}, f32[6,8,128]{2,1,0:T(8,128)S(1)}, u32[]{:S(2)}, u32[]{:S(2)}) collective-permute-start(f32[6,8,128]{2,1,0:T(8,128)S(1)} %get-tuple-element.878), channel_id=1, source_target_pairs={{0,28},{4,0},{8,4},{12,8},{16,12},{20,16},{24,20},{28,24},{1,29},{... | collective-permute-start | bytes 73736 | tf_op jit(solution)/shard_map/ppermute | solution.py:18
  121.4 4.2 %collective-permute-start.5 = (f32[6,8,128]{2,1,0:T(8,128)S(1)}, f32[6,8,128]{2,1,0:T(8,128)S(1)}, u32[]{:S(2)}, u32[]{:S(2)}) collective-permute-start(f32[6,8,128]{2,1,0:T(8,128)S(1)} %get-tuple-element.877), channel_id=1, source_target_pairs={{0,4},{4,8},{8,12},{12,16},{16,20},{20,24},{24,28},{28,0},{1,5},{5... | collective-permute-start | bytes 73736 | tf_op jit(solution)/shard_map/ppermute | solution.py:18
  126.0 5.1 %collective-permute-start.6 = (f32[6,8,8]{2,1,0:T(8,128)S(1)}, f32[6,8,8]{2,1,0:T(8,128)S(1)}, u32[]{:S(2)}, u32[]{:S(2)}) collective-permute-start(f32[6,8,8]{2,1,0:T(8,128)S(1)} %constant_dynamic-update-slice_fusion.62), channel_id=1, source_target_pairs={{0,3},{1,0},{2,1},{3,2},{4,7},{5,4},{6,5},{7,6},{8,11},{9,8},{10,9... | collective-permute-start | bytes 4616 | tf_op jit(solution)/shard_map/ppermute | solution.py:18
  129.8 5.9 %collective-permute-start.7 = (f32[6,8,8]{2,1,0:T(8,128)S(1)}, f32[6,8,8]{2,1,0:T(8,128)S(1)}, u32[]{:S(2)}, u32[]{:S(2)}) collective-permute-start(f32[6,8,8]{2,1,0:T(8,128)S(1)} %constant_dynamic-update-slice_fusion.68), channel_id=1, source_target_pairs={{0,1},{1,2},{2,3},{3,0},{4,5},{5,6},{6,7},{7,4},{8,9},{9,10},{10,1... | collective-permute-start | bytes 4616 | tf_op jit(solution)/shard_map/ppermute | solution.py:18
  176.5 4.5 %collective-permute-start.9 = (f32[6,8,128]{2,1,0:T(8,128)S(1)}, f32[6,8,128]{2,1,0:T(8,128)S(1)}, u32[]{:S(2)}, u32[]{:S(2)}) collective-permute-start(f32[6,8,128]{2,1,0:T(8,128)S(1)} %get-tuple-element.866), channel_id=1, source_target_pairs={{0,4},{4,8},{8,12},{12,16},{16,20},{20,24},{24,28},{28,0},{1,5},{5... | collective-permute-start | bytes 73736 | tf_op jit(solution)/shard_map/ppermute | solution.py:18
  177.0 4.2 %collective-permute-start.8 = (f32[6,8,128]{2,1,0:T(8,128)S(1)}, f32[6,8,128]{2,1,0:T(8,128)S(1)}, u32[]{:S(2)}, u32[]{:S(2)}) collective-permute-start(f32[6,8,128]{2,1,0:T(8,128)S(1)} %get-tuple-element.867), channel_id=1, source_target_pairs={{0,28},{4,0},{8,4},{12,8},{16,12},{20,16},{24,20},{28,24},{1,29},{... | collective-permute-start | bytes 73736 | tf_op jit(solution)/shard_map/ppermute | solution.py:18
  181.3 3.9 %collective-permute-start.10 = (f32[6,8,8]{2,1,0:T(8,128)S(1)}, f32[6,8,8]{2,1,0:T(8,128)S(1)}, u32[]{:S(2)}, u32[]{:S(2)}) collective-permute-start(f32[6,8,8]{2,1,0:T(8,128)S(1)} %constant_dynamic-update-slice_fusion.112), channel_id=1, source_target_pairs={{0,3},{1,0},{2,1},{3,2},{4,7},{5,4},{6,5},{7,6},{8,11},{9,8},{10,9... | collective-permute-start | bytes 4616 | tf_op jit(solution)/shard_map/ppermute | solution.py:18
  181.9 5.7 %collective-permute-start.11 = (f32[6,8,8]{2,1,0:T(8,128)S(1)}, f32[6,8,8]{2,1,0:T(8,128)S(1)}, u32[]{:S(2)}, u32[]{:S(2)}) collective-permute-start(f32[6,8,8]{2,1,0:T(8,128)S(1)} %constant_dynamic-update-slice_fusion.118), channel_id=1, source_target_pairs={{0,1},{1,2},{2,3},{3,0},{4,5},{5,6},{6,7},{7,4},{8,9},{9,10},{10,1... | collective-permute-start | bytes 4616 | tf_op jit(solution)/shard_map/ppermute | solution.py:18
  190.0 0.9 copy-start.38
  232.2 0.7 copy-start.39
where the time goes:
time: 237 us; the launch traced here: 233 us
  local copies, waits for them, and re-layouts  89.8 us (38%)
  matrix products  55.1 us (23%)
  other arithmetic  53.5 us (23%)
  starting transfers between devices  17.2 us (7%)
  waiting for transfers between devices  11.9 us (5%)
  loops' own time  3.4 us (1%)
    dot_general x48, matrix products, collide(): jnp.tensordot(jnp.asarray(speeds.T), fluid, axes=1, precision=lax.Precisi...  34.9 us
    unnamed x148, local copies, waits for them, and re-layouts  30.7 us
    reduce_sum x24, other arithmetic, collide(): density = jnp.sum(fluid, axis=0)  21.9 us
    ppermute x12, starting transfers between devices, from_behind(): return lax.ppermute(value, axis, pairs)  17.2 us
    dot_general x48, matrix products, collide(): jnp.tensordot(jnp.asarray(speeds), velocity, axes=1, precision=lax.Precis...  13.9 us
    reduce_sum x24, other arithmetic, collide(): amount = jnp.sum(tracer, axis=0)  12.3 us
    ppermute x12, waiting for transfers between devices, from_behind(): return lax.ppermute(value, axis, pairs)  11.9 us
    slice x18, local copies, waits for them, and re-layouts, pull_leaving(): field[:, :, 1:]  11.3 us
  transfers between devices with their start and end apart: 12, of which 6 were waited for; matrix products, arithmetic and copies ran while one was open for 25% of the time, Pallas kernels for 0%

commit v1 on v0

v1 whole, which is shorter than its diff:
```python
import functools

import jax
import jax.numpy as jnp
from jax import lax
from jax.experimental import pallas as pl
from jax.experimental.pallas import tpu as pltpu
from jax.sharding import PartitionSpec as P

TRACER_RATE = 1.3
ADSORB = 0.3
FLOW = [
    (0, 0, 0), (1, 0, 0), (-1, 0, 0), (0, 1, 0), (0, -1, 0), (0, 0, 1), (0, 0, -1),
    (1, 1, 0), (-1, -1, 0), (1, -1, 0), (-1, 1, 0), (1, 0, 1), (-1, 0, -1), (1, 0, -1),
    (-1, 0, 1), (0, 1, 1), (0, -1, -1), (0, 1, -1), (0, -1, 1),
]
SPEEDS = FLOW + FLOW[:7]
COUNT = len(SPEEDS)
X_LISTS = [[1, 7, 9, 11, 13, 20], [2, 8, 10, 12, 14, 21]]
Y_LISTS = [[3, 7, 10, 15, 17, 22], [4, 8, 9, 16, 18, 23]]
CORNERS = [7, 8, 9, 10]
MESH = pl.DeviceIdType.MESH
SLOT = 16


def macros(f, h):
    s = [f[2 * k - 1] + f[2 * k] for k in range(1, 10)]
    d = [f[2 * k - 1] - f[2 * k] for k in range(1, 10)]
    rho = f[0] + ((s[0] + s[1]) + (s[2] + s[3])) + ((s[4] + s[5]) + (s[6] + s[7])) + s[8]
    inv = 1.0 / rho
    ux = (d[0] + (d[3] + d[4]) + (d[5] + d[6])) * inv
    uy = (d[1] + (d[3] - d[4]) + (d[7] + d[8])) * inv
    uz = (d[2] + (d[5] - d[6]) + (d[7] - d[8])) * inv
    amount = h[0] + ((h[1] + h[2]) + (h[3] + h[4])) + (h[5] + h[6])
    return ux, uy, uz, amount * inv * (4.0 * TRACER_RATE * 0.125)


def transpose_collision(p, q, ux, uy, uz, cr, label):
    s = [None] + [p[2 * k - 1] + p[2 * k] for k in range(1, 10)]
    d = [None] + [p[2 * k - 1] - p[2 * k] for k in range(1, 10)]
    kept = jnp.where(label == 2, 1.0 - ADSORB, 1.0)
    tx, ty, tz = q[1] - q[2], q[3] - q[4], q[5] - q[6]
    crk = cr * kept
    bx, by, bz = crk * tx, crk * ty, crk * tz
    total = ((q[1] + q[2]) + (q[3] + q[4])) + (q[5] + q[6])
    drift = ux * tx + uy * ty + uz * tz
    common = (kept * TRACER_RATE) * (0.25 * q[0] + 0.125 * total + 0.5 * drift)
    direct = kept * (1.0 - TRACER_RATE)
    h_out = [direct * value + common for value in q]
    sxy, dxy = s[4] + s[5], s[4] - s[5]
    sxz, dxz = s[6] + s[7], s[6] - s[7]
    syz, dyz = s[8] + s[9], s[8] - s[9]
    axis_sum = (s[1] + s[2]) + s[3]
    edge_sum = (sxy + sxz) + syz
    ce, cs = 1.19 / 2394.0, 1.4 / 252.0
    te = (8.0 * ce) * edge_sum - (11.0 * ce) * axis_sum - (30.0 * ce) * p[0]
    ts = cs * edge_sum - (4.0 * cs) * axis_sum + (12.0 * cs) * p[0]
    rx, ry, rz = s[1] - syz, s[2] - sxz, s[3] - sxy
    r_third = (axis_sum - edge_sum) * (1.0 / 3.0)
    gx, gy, gz = 2.0 * s[1] + syz, 2.0 * s[2] + sxz, 2.0 * s[3] + sxy
    g_third = (2.0 * axis_sum + edge_sum) * (1.0 / 3.0)
    cp, cq = 1.25 * 6.0 / 36.0, 1.4 * 6.0 / 72.0
    px, py, pz = cp * (rx - r_third), cp * (ry - r_third), cp * (rz - r_third)
    wx, wy, wz = cq * (gx - g_third), cq * (gy - g_third), cq * (gz - g_third)
    txy, txz, tyz = (1.25 / 4.0) * dxy, (1.25 / 4.0) * dxz, (1.25 / 4.0) * dyz
    base = 38.0 * te - 11.0 * ts
    sx = base + 2.0 * px + wx
    sy = base + 2.0 * py + wy
    sz = base + 2.0 * pz + wz
    vx = sx * ux + txy * uy + txz * uz
    vy = txy * ux + sy * uy + tyz * uz
    vz = txz * ux + tyz * uy + sz * uz
    nx, ny, nz = vx + bx, vy + by, vz + bz
    shift = ux * (nx - 0.5 * vx) + uy * (ny - 0.5 * vy) + uz * (nz - 0.5 * vz)
    e0 = 9.0 * ts - 19.0 * te + shift
    ea = shift - 7.0 * ts
    ee = 19.0 * te - 2.0 * ts + shift
    even_axis = [ea + px + 2.0 * wx, ea + py + 2.0 * wy, ea + pz + 2.0 * wz]
    exy, exz, eyz = ee - pz + wz, ee - py + wy, ee - px + wx
    axy, bxy = d[4] + d[5], d[4] - d[5]
    axz, bxz = d[6] + d[7], d[6] - d[7]
    ayz, byz = d[8] + d[9], d[8] - d[9]
    ck, cm = 1.2 / 40.0, 1.98 / 8.0
    kx = ck * ((axy + axz) - 4.0 * d[1])
    ky = ck * ((bxy + ayz) - 4.0 * d[2])
    kz = ck * ((bxz + byz) - 4.0 * d[3])
    mx, my, mz = cm * (axy - axz), cm * (ayz - bxy), cm * (bxz - byz)
    jx, jy, jz = (5.0 / 3.0) * kx - nx, (5.0 / 3.0) * ky - ny, (5.0 / 3.0) * kz - nz
    odd_axis = [jx - 5.0 * kx, jy - 5.0 * ky, jz - 5.0 * kz]
    xp, xm, yp, ym, zp, zm = jx + mx, jx - mx, jy + my, jy - my, jz + mz, jz - mz
    even = even_axis + [exy + txy, exy - txy, exz + txz, exz - txz, eyz + tyz, eyz - tyz]
    odd = odd_axis + [xp + ym, xp - ym, xm + zp, xm - zp, yp + zm, yp - zm]
    solid = label == 1
    f_out = [jnp.where(solid, p[0], p[0] - e0)]
    for k in range(9):
        up, down = p[2 * k + 1], p[2 * k + 2]
        f_out.append(jnp.where(solid, down, up - (even[k] + odd[k])))
        f_out.append(jnp.where(solid, up, down - (even[k] - odd[k])))
    h_final = [jnp.where(solid, q[0], h_out[0])]
    for k in range(3):
        h_final.append(jnp.where(solid, q[2 * k + 2], h_out[2 * k + 1]))
        h_final.append(jnp.where(solid, q[2 * k + 1], h_out[2 * k + 2]))
    return f_out, h_final


def kernel(
    sf_hbm, st_hbm, af_hbm, at_hbm, lab_hbm, of_hbm, ot_hbm,
    sf, st, lab, field, macro, send_x, recv_x, send_y, recv_y, recv_c,
    in_sem, out_sem, send_sem, recv_sem,
):
    nx, ny = lax.axis_size("gx"), lax.axis_size("gy")
    mx, my = lax.axis_index("gx"), lax.axis_index("gy")
    steps, planes = sf.shape[0], sf.shape[2]
    rows, lanes = sf.shape[3], sf.shape[4]
    flow = sf.shape[1]
    x_next, x_prior = lax.rem(mx + 1, nx), lax.rem(mx + nx - 1, nx)
    y_next, y_prior = lax.rem(my + 1, ny), lax.rem(my + ny - 1, ny)
    neighbours = [
        (x_prior, my), (x_next, my), (mx, y_prior), (mx, y_next),
        (x_prior, y_prior), (x_next, y_next), (x_prior, y_next), (x_next, y_prior),
    ]
    barrier = pltpu.get_barrier_semaphore()
    for device in neighbours:
        pl.semaphore_signal(barrier, inc=1, device_id=device, device_id_type=MESH)

    loads = [
        pltpu.make_async_copy(af_hbm, field.at[0, pl.ds(0, flow)], in_sem.at[0]),
        pltpu.make_async_copy(at_hbm, field.at[0, pl.ds(flow, COUNT - flow)], in_sem.at[1]),
        pltpu.make_async_copy(sf_hbm, sf, in_sem.at[2]),
        pltpu.make_async_copy(st_hbm, st, in_sem.at[3]),
        pltpu.make_async_copy(lab_hbm, lab, in_sem.at[4]),
    ]
    for load in loads:
        load.start()

    lane = lax.broadcasted_iota(jnp.int32, (rows, lanes), 1)
    row = lax.broadcasted_iota(jnp.int32, (rows, lanes), 0)
    ends = [lane == 0, lane == lanes - 1]
    edges = [row == rows - 1, row == 0]

    def insert(packed, values):
        done = []
        for side in range(2):
            acc = pltpu.roll(packed[side], lanes - SLOT, 1)
            for k, number in enumerate(Y_LISTS[side]):
                target = lanes - SLOT + k
                moved = pltpu.roll(values[number], target + side, 1)
                acc = jnp.where(lane == target, moved, acc)
            done.append(acc)
        return tuple(done)

    def send(step, source):
        for side in range(2):
            at = 0 if side == 0 else rows - 1
            for k, number in enumerate(X_LISTS[side]):
                send_x[step, side, k] = field[source, number, :, at, :]
        pairs = [
            (send_x.at[step, 0], recv_x.at[step, 0]),
            (send_x.at[step, 1], recv_x.at[step, 1]),
            (send_y.at[step, 0], recv_y.at[step, 0]),
            (send_y.at[step, 1], recv_y.at[step, 1]),
            (send_x.at[step, 0, 1], recv_c.at[step, 0]),
            (send_x.at[step, 1, 1], recv_c.at[step, 1]),
            (send_x.at[step, 0, 2], recv_c.at[step, 2]),
            (send_x.at[step, 1, 2], recv_c.at[step, 3]),
        ]
        copies = []
        for number, ((source_ref, target_ref), device) in enumerate(zip(pairs, neighbours)):
            copies.append(
                pltpu.make_async_remote_copy(
                    src_ref=source_ref,
                    dst_ref=target_ref,
                    send_sem=send_sem.at[step, number],
                    recv_sem=recv_sem.at[step, number],
                    device_id=device,
                    device_id_type=MESH,
                )
            )
        for copy in copies:
            copy.start()
        return copies

    loads[0].wait()
    loads[1].wait()

    def first_pack(z, packed):
        values = {n: field[0, n, z] for side in Y_LISTS for n in side}
        return insert(packed, values)

    empty = (jnp.zeros((rows, lanes), jnp.float32),) * 2
    packed = lax.fori_loop(0, planes, first_pack, empty)
    send_y[0, 0] = packed[0]
    send_y[0, 1] = packed[1]
    pl.semaphore_wait(barrier, len(neighbours))
    started = [send(0, 0)]
    for load in loads[2:]:
        load.wait()

    def prepare(index, carry):
        step, z = index // planes, index % planes
        f = [sf[step, n, z].astype(jnp.float32) for n in range(flow)]
        h = [st[step, n, z].astype(jnp.float32) for n in range(COUNT - flow)]
        for k, value in enumerate(macros(f, h)):
            macro[step, k, z] = value
        return carry

    lax.fori_loop(0, steps * planes, prepare, 0)

    stores = []
    for step in range(steps):
        saved = steps - 1 - step
        source, target = step % 2, (step + 1) % 2
        for copy in started[step]:
            copy.wait_recv()
        for corner, number in enumerate(CORNERS):
            side = 0 if SPEEDS[number][0] == 1 else 1
            end = ends[0] if SPEEDS[number][1] == 1 else ends[1]
            k = X_LISTS[side].index(number)
            recv_x[step, side, k] = jnp.where(end, recv_c[step, corner], recv_x[step, side, k])
        last = step == steps - 1

        def plane(z, carry):
            got, packed = carry
            pulled = []
            for number in range(COUNT):
                cx, cy, cz = SPEEDS[number]
                zz = lax.rem(z + (cz + planes), planes) if cz else z
                value = field[source, number, zz]
                if cy:
                    side = 0 if cy == 1 else 1
                    at = (SLOT * cz) % lanes + Y_LISTS[side].index(number)
                    to = 0 if cy == 1 else lanes - 1
                    column = pltpu.roll(got[side], (to - at) % lanes, 1)
                    value = jnp.where(ends[side], column, value)
                if cx:
                    side = 0 if cx == 1 else 1
                    k = X_LISTS[side].index(number)
                    value = pltpu.roll(value, rows - 1 if cx == 1 else 1, 0)
                    halo = jnp.broadcast_to(recv_x[step, side, k, pl.ds(zz, 1), :], (rows, lanes))
                    value = jnp.where(edges[side], halo, value)
                if cy:
                    value = pltpu.roll(value, lanes - 1 if cy == 1 else 1, 1)
                pulled.append(value)
            ux, uy, uz, cr = [macro[saved, k, z] for k in range(4)]
            f_out, h_out = transpose_collision(
                pulled[:flow], pulled[flow:], ux, uy, uz, cr, lab[z]
            )
            values = f_out + h_out
            for number in range(COUNT):
                field[target, number, z] = values[number]
            if last:
                return got, packed
            got = tuple(pltpu.roll(value, lanes - SLOT, 1) for value in got)
            return got, insert(packed, values)

        def last_plane(z, carry):
            carry = plane(z, carry)
            got, packed = carry
            got = tuple(pltpu.roll(value, lanes - SLOT, 1) for value in got)
            return got, packed

        got = (recv_y[step, 0], recv_y[step, 1])
        got, packed = lax.fori_loop(0, planes, last_plane if last else plane, (got, empty))
        if not last:
            send_y[step + 1, 0] = packed[0]
            send_y[step + 1, 1] = packed[1]
            started.append(send(step + 1, target))
    final = steps % 2
    stores = [
        pltpu.make_async_copy(field.at[final, pl.ds(0, flow)], of_hbm, out_sem.at[0]),
        pltpu.make_async_copy(field.at[final, pl.ds(flow, COUNT - flow)], ot_hbm, out_sem.at[1]),
    ]
    for store in stores:
        store.start()
    for copies in started:
        for copy in copies:
            copy.wait_send()
    for store in stores:
        store.wait()


def body(saved_fluid, saved_tracer, adjoint_fluid, adjoint_tracer, label):
    steps, flow, planes, rows, lanes = saved_fluid.shape
    tracer = saved_tracer.shape[1]
    f32 = jnp.float32
    tile = (rows, lanes)
    return pl.pallas_call(
        kernel,
        out_shape=(
            jax.ShapeDtypeStruct(adjoint_fluid.shape, f32),
            jax.ShapeDtypeStruct(adjoint_tracer.shape, f32),
        ),
        in_specs=[pl.BlockSpec(memory_space=pl.ANY)] * 5,
        out_specs=[pl.BlockSpec(memory_space=pl.ANY)] * 2,
        scratch_shapes=[
            pltpu.VMEM(saved_fluid.shape, saved_fluid.dtype),
            pltpu.VMEM(saved_tracer.shape, saved_tracer.dtype),
            pltpu.VMEM(label.shape, label.dtype),
            pltpu.VMEM((2, flow + tracer, planes) + tile, f32),
            pltpu.VMEM((steps, 4, planes) + tile, f32),
            pltpu.VMEM((steps, 2, 6, planes, lanes), f32),
            pltpu.VMEM((steps, 2, 6, planes, lanes), f32),
            pltpu.VMEM((steps, 2) + tile, f32),
            pltpu.VMEM((steps, 2) + tile, f32),
            pltpu.VMEM((steps, 4, planes, lanes), f32),
            pltpu.SemaphoreType.DMA((5,)),
            pltpu.SemaphoreType.DMA((2,)),
            pltpu.SemaphoreType.DMA((steps, 8)),
            pltpu.SemaphoreType.DMA((steps, 8)),
        ],
        compiler_params=pltpu.CompilerParams(
            collective_id=0, has_side_effects=True, vmem_limit_bytes=32 * 1024 * 1024
        ),
        name="adjoint_steps",
    )(saved_fluid, saved_tracer, adjoint_fluid, adjoint_tracer, label)


def solution(mesh):
    placed = (
        P(None, None, None, "gx", "gy"),
        P(None, None, None, "gx", "gy"),
        P(None, None, "gx", "gy"),
        P(None, None, "gx", "gy"),
        P(None, "gx", "gy"),
    )
    return jax.shard_map(
        body,
        mesh=mesh,
        in_specs=placed,
        out_specs=(P(None, None, "gx", "gy"), P(None, None, "gx", "gy")),
        check_vma=False,
    )
```

time: 237 us -> 31.7 us (0.13); the launches traced: 233 us -> 31.4 us
  local copies, waits for them, and re-layouts: 89.8 us -> 6.44 us
  matrix products: 55.1 us -> 0 us
  other arithmetic: 53.5 us -> 0 us
  Pallas kernels: 0 us -> 24.3 us
  starting transfers between devices: 17.2 us -> 0 us
  waiting for transfers between devices: 11.9 us -> 0 us
  loops' own time: 3.4 us -> 0 us
    dot_general x120 -> x0, matrix products: 55.1 us -> none  [the longest x48 34.9 us: collide(): jnp.tensordot(jnp.asarray(speeds.T), fluid, axes=1, precision=lax.Precisi...]
    slice x108 -> x0, local copies, waits for them, and re-layouts: 35 us -> none  [the longest x18 11.3 us: pull_leaving(): field[:, :, 1:]]
    reduce_sum x48 -> x0, other arithmetic: 34.2 us -> none  [the longest x24 21.9 us: collide(): density = jnp.sum(fluid, axis=0)]
    pallas_call x0 -> x1, Pallas kernels: none -> 24.3 us  [body(): pl.pallas_call(kernel, out_shape=(jax.ShapeDtypeStruct(adjoint_fluid.shap...]
    unnamed x148 -> x12, local copies, waits for them, and re-layouts: 30.7 us -> 6.44 us
    ppermute x12 -> x0, starting transfers between devices: 17.2 us -> none  [from_behind(): return lax.ppermute(value, axis, pairs)]
    ppermute x12 -> x0, waiting for transfers between devices: 11.9 us -> none  [from_behind(): return lax.ppermute(value, axis, pairs)]
    another operation x112 -> x0, local copies, waits for them, and re-layouts: 11.4 us -> none  [the longest x21 3.01 us: pull_leaving(): from_above[NEXT_ROWS.index(number)][:, :, None]]
  transfers between devices with their start and end apart: 12 -> 0, of which waited for: 6 -> 0; matrix products, arithmetic and copies ran while one was open for 25% -> 0% of each run, Pallas kernels for 0% -> 0%
where the time goes in v1:
time: 31.7 us; the launch traced here: 31.4 us
  Pallas kernels  24.3 us (77%)
  local copies, waits for them, and re-layouts  6.44 us (20%)
  between operations  0.65 us (2%)
    pallas_call x1, Pallas kernels, body(): pl.pallas_call(kernel, out_shape=(jax.ShapeDtypeStruct(adjoint_fluid.shap...  24.3 us
    unnamed x12, local copies, waits for them, and re-layouts  6.44 us

profile of v1, /device:TPU:0, one launch (start us, length us, event | category | flops | bytes accessed | tf_op | source)
XLA Modules:
  0.0 31.4 jit_solution(5062939932361834243)
XLA Ops:
  0.6 0.0 copy-start
  0.6 1.2 %copy-done = bf16[3,19,8,8,128]{4,3,2,1,0:T(8,128)(2,1)S(1)} copy-done((bf16[3,19,8,8,128]{4,3,2,1,0:T(8,128)(2,1)S(1)}, bf16[3,19,8,8,128]{4,3,2,1,0:T(8,128)(2,1)}, u32[]{:S(2)}) %copy-start) | copy-done | bytes 933912
  1.8 0.0 copy-start.1
  1.8 1.1 %copy-done.1 = f32[19,8,8,128]{3,2,1,0:T(8,128)S(1)} copy-done((f32[19,8,8,128]{3,2,1,0:T(8,128)S(1)}, f32[19,8,8,128]{3,2,1,0:T(8,128)}, u32[]{:S(2)}) %copy-start.1) | copy-done | bytes 622616
  2.9 0.0 copy-start.2
  2.9 1.0 %copy-done.2 = bf16[3,7,8,8,128]{4,3,2,1,0:T(8,128)(2,1)S(1)} copy-done((bf16[3,7,8,8,128]{4,3,2,1,0:T(8,128)(2,1)S(1)}, bf16[3,7,8,8,128]{4,3,2,1,0:T(8,128)(2,1)}, u32[]{:S(2)}) %copy-start.2) | copy-done | bytes 344088
  3.9 0.0 copy-start.3
  3.9 0.9 %copy-done.3 = f32[7,8,8,128]{3,2,1,0:T(8,128)S(1)} copy-done((f32[7,8,8,128]{3,2,1,0:T(8,128)S(1)}, f32[7,8,8,128]{3,2,1,0:T(8,128)}, u32[]{:S(2)}) %copy-start.3) | copy-done | bytes 229400
  4.8 0.0 copy-start.4
  4.8 0.8 %copy-done.4 = s32[8,8,128]{2,1,0:T(8,128)S(1)} copy-done((s32[8,8,128]{2,1,0:T(8,128)S(1)}, s32[8,8,128]{2,1,0:T(8,128)}, u32[]{:S(2)}) %copy-start.4) | copy-done | bytes 32792
  5.6 24.3 %adjoint_steps.1 = (f32[19,8,8,128]{3,2,1,0:T(8,128)S(1)}, f32[7,8,8,128]{3,2,1,0:T(8,128)S(1)}) custom-call(bf16[3,19,8,8,128]{4,3,2,1,0:T(8,128)(2,1)S(1)} %copy-done, bf16[3,7,8,8,128]{4,3,2,1,0:T(8,128)(2,1)S(1)} %copy-done.2, f32[19,8,8,128]{3,2,1,0:T(8,128)S(1)} %copy-done.1, f32[7,8,8,128]{3,2,1,0:T(8,128)S(1)} %copy-done.3, s32[8,8,128]{2,1,0:T(8,128)S(1)} %copy-done.4), custom_call_target="tpu_custom_call" | custom-call | tf_op jit(solution)/shard_map/adjoint_steps/pallas_call | solution.py:287
  29.9 0.8 %copy.9 = f32[19,8,8,128]{3,2,1,0:T(8,128)} copy(f32[19,8,8,128]{3,2,1,0:T(8,128)S(1)} %get-tuple-element.4) | data formatting | bytes 1245184
  30.7 0.7 %copy.10 = f32[7,8,8,128]{3,2,1,0:T(8,128)} copy(f32[7,8,8,128]{3,2,1,0:T(8,128)S(1)} %get-tuple-element.5) | data formatting | bytes 458752
Async XLA Ops:
  0.6 1.2 %copy-start = (bf16[3,19,8,8,128]{4,3,2,1,0:T(8,128)(2,1)S(1)}, bf16[3,19,8,8,128]{4,3,2,1,0:T(8,128)(2,1)}, u32[]{:S(2)}) copy-start(bf16[3,19,8,8,128]{4,3,2,1,0:T(8,128)(2,1)} %sf_hbm.1) | copy-start | bytes 2801668
  1.8 1.1 %copy-start.1 = (f32[19,8,8,128]{3,2,1,0:T(8,128)S(1)}, f32[19,8,8,128]{3,2,1,0:T(8,128)}, u32[]{:S(2)}) copy-start(f32[19,8,8,128]{3,2,1,0:T(8,128)} %af_hbm.1) | copy-start | bytes 1867780
  2.9 1.0 %copy-start.2 = (bf16[3,7,8,8,128]{4,3,2,1,0:T(8,128)(2,1)S(1)}, bf16[3,7,8,8,128]{4,3,2,1,0:T(8,128)(2,1)}, u32[]{:S(2)}) copy-start(bf16[3,7,8,8,128]{4,3,2,1,0:T(8,128)(2,1)} %st_hbm.1) | copy-start | bytes 1032196
  3.9 0.9 %copy-start.3 = (f32[7,8,8,128]{3,2,1,0:T(8,128)S(1)}, f32[7,8,8,128]{3,2,1,0:T(8,128)}, u32[]{:S(2)}) copy-start(f32[7,8,8,128]{3,2,1,0:T(8,128)} %at_hbm.1) | copy-start | bytes 688132
  4.8 0.8 %copy-start.4 = (s32[8,8,128]{2,1,0:T(8,128)S(1)}, s32[8,8,128]{2,1,0:T(8,128)}, u32[]{:S(2)}) copy-start(s32[8,8,128]{2,1,0:T(8,128)} %lab_hbm.1) | copy-start | bytes 98308

commit v2 on v1

--- a/solution.py
+++ b/solution.py
@@ -188,7 +188,7 @@
         return insert(packed, values)
 
     empty = (jnp.zeros((rows, lanes), jnp.float32),) * 2
-    packed = lax.fori_loop(0, planes, first_pack, empty)
+    packed = lax.fori_loop(0, planes, first_pack, empty, unroll=8)
     send_y[0, 0] = packed[0]
     send_y[0, 1] = packed[1]
     pl.semaphore_wait(barrier, len(neighbours))
@@ -204,7 +204,7 @@
             macro[step, k, z] = value
         return carry
 
-    lax.fori_loop(0, steps * planes, prepare, 0)
+    lax.fori_loop(0, steps * planes, prepare, 0, unroll=4)
 
     stores = []
     for step in range(steps):
@@ -260,7 +260,7 @@
             return got, packed
 
         got = (recv_y[step, 0], recv_y[step, 1])
-        got, packed = lax.fori_loop(0, planes, last_plane if last else plane, (got, empty))
+        got, packed = lax.fori_loop(0, planes, last_plane if last else plane, (got, empty), unroll=8)
         if not last:
             send_y[step + 1, 0] = packed[0]
             send_y[step + 1, 1] = packed[1]
@@ -309,7 +309,7 @@
             pltpu.SemaphoreType.DMA((steps, 8)),
         ],
         compiler_params=pltpu.CompilerParams(
-            collective_id=0, has_side_effects=True, vmem_limit_bytes=32 * 1024 * 1024
+            collective_id=0, has_side_effects=True, vmem_limit_bytes=60 * 1024 * 1024
         ),
         name="adjoint_steps",
     )(saved_fluid, saved_tracer, adjoint_fluid, adjoint_tracer, label)

time: 31.7 us -> 25.4 us (0.80)
  local copies, waits for them, and re-layouts: 6.44 us -> 2.69 us
  Pallas kernels: 24.3 us -> 21.9 us
    unnamed x12 -> x4, local copies, waits for them, and re-layouts: 6.44 us -> 2.69 us
    pallas_call x1, Pallas kernels: 24.3 us -> 21.9 us  [body(): pl.pallas_call(kernel, out_shape=(jax.ShapeDtypeStruct(adjoint_fluid.shap...]
where the time goes in v2:
time: 25.4 us; the launch traced here: 25.2 us
  Pallas kernels  21.9 us (86%)
  local copies, waits for them, and re-layouts  2.69 us (11%)
  between operations  0.65 us (3%)
    pallas_call x1, Pallas kernels, body(): pl.pallas_call(kernel, out_shape=(jax.ShapeDtypeStruct(adjoint_fluid.shap...  21.9 us
    unnamed x4, local copies, waits for them, and re-layouts  2.69 us

profile of v2, /device:TPU:0, one launch (start us, length us, event | category | flops | bytes accessed | tf_op | source)
XLA Modules:
  0.0 25.2 jit_solution(11417172860436741785)
XLA Ops:
  0.6 21.9 %adjoint_steps.1 = (f32[19,8,8,128]{3,2,1,0:T(8,128)}, f32[7,8,8,128]{3,2,1,0:T(8,128)}) custom-call(bf16[3,19,8,8,128]{4,3,2,1,0:T(8,128)(2,1)} %sf_hbm.1, bf16[3,7,8,8,128]{4,3,2,1,0:T(8,128)(2,1)} %st_hbm.1, f32[19,8,8,128]{3,2,1,0:T(8,128)} %af_hbm.1, f32[7,8,8,128]{3,2,1,0:T(8,128)} %at_hbm.1, s32[8,8,128]{2,1,0:T(8,128)} %lab_hbm.1), custom_call_target="tpu_custom_call" | custom-call | tf_op jit(solution)/shard_map/adjoint_steps/pallas_call | solution.py:287
  22.5 0.0 copy-start
  22.5 2.0 %copy.9 = f32[19,8,8,128]{3,2,1,0:T(8,128)} copy(f32[19,8,8,128]{3,2,1,0:T(8,128)} %get-tuple-element.4) | data formatting | bytes 1245184
  24.5 0.0 copy-done
  24.5 0.7 %copy.10 = f32[7,8,8,128]{3,2,1,0:T(8,128)} copy(f32[7,8,8,128]{3,2,1,0:T(8,128)S(1)} %copy-done) | data formatting | bytes 458752
Async XLA Ops:
  22.5 2.0 %copy-start = (f32[7,8,8,128]{3,2,1,0:T(8,128)S(1)}, f32[7,8,8,128]{3,2,1,0:T(8,128)}, u32[]{:S(2)}) copy-start(f32[7,8,8,128]{3,2,1,0:T(8,128)} %get-tuple-element.5) | copy-start | bytes 688132

commit v3 on v2

--- a/solution.py
+++ b/solution.py
@@ -21,6 +21,8 @@
 CORNERS = [7, 8, 9, 10]
 MESH = pl.DeviceIdType.MESH
 SLOT = 16
+IN_SPACE = pltpu.HBM
+FIRST_VMEM = 32 * 1024 * 1024
 
 
 def macros(f, h):
@@ -103,10 +105,42 @@
     return f_out, h_final
 
 
+def tiles(rows, lanes):
+    lane = lax.broadcasted_iota(jnp.int32, (rows, lanes), 1)
+    row = lax.broadcasted_iota(jnp.int32, (rows, lanes), 0)
+    return lane, [lane == 0, lane == lanes - 1], [row == rows - 1, row == 0]
+
+
+def pull_plane(z, field, halo_x, got, ends, edges):
+    planes, rows, lanes = field.shape[1:]
+    pulled = []
+    for number in range(COUNT):
+        cx, cy, cz = SPEEDS[number]
+        zz = lax.rem(z + (cz + planes), planes) if cz else z
+        value = field[number, zz]
+        if cy:
+            side = 0 if cy == 1 else 1
+            at = (SLOT * cz) % lanes + Y_LISTS[side].index(number)
+            to = 0 if cy == 1 else lanes - 1
+            column = pltpu.roll(got[side], (to - at) % lanes, 1)
+            value = jnp.where(ends[side], column, value)
+        if cx:
+            side = 0 if cx == 1 else 1
+            k = X_LISTS[side].index(number)
+            value = pltpu.roll(value, rows - 1 if cx == 1 else 1, 0)
+            halo = jnp.broadcast_to(halo_x[side, k, pl.ds(zz, 1), :], (rows, lanes))
+            value = jnp.where(edges[side], halo, value)
+        if cy:
+            value = pltpu.roll(value, lanes - 1 if cy == 1 else 1, 1)
+        pulled.append(value)
+    return pulled
+
+
 def kernel(
-    sf_hbm, st_hbm, af_hbm, at_hbm, lab_hbm, of_hbm, ot_hbm,
-    sf, st, lab, field, macro, send_x, recv_x, send_y, recv_y, recv_c,
-    in_sem, out_sem, send_sem, recv_sem,
+    sf_hbm, st_hbm, af_hbm, at_hbm, lab_hbm,
+    field_out, macro_out, halo_x_out, halo_y_out, lab,
+    sf, st, field, macro, send_x, recv_x, send_y, recv_y, recv_c,
+    in_sem, send_sem, recv_sem,
 ):
     nx, ny = lax.axis_size("gx"), lax.axis_size("gy")
     mx, my = lax.axis_index("gx"), lax.axis_index("gy")
@@ -133,11 +167,7 @@
     for load in loads:
         load.start()
 
-    lane = lax.broadcasted_iota(jnp.int32, (rows, lanes), 1)
-    row = lax.broadcasted_iota(jnp.int32, (rows, lanes), 0)
-    ends = [lane == 0, lane == lanes - 1]
-    edges = [row == rows - 1, row == 0]
-
+    lane, ends, edges = tiles(rows, lanes)
     def insert(packed, values):
         done = []
         for side in range(2):
@@ -153,7 +183,7 @@
         for side in range(2):
             at = 0 if side == 0 else rows - 1
             for k, number in enumerate(X_LISTS[side]):
-                send_x[step, side, k] = field[source, number, :, at, :]
+                send_x[step, side, k] = source[number, :, at, :]
         pairs = [
             (send_x.at[step, 0], recv_x.at[step, 0]),
             (send_x.at[step, 1], recv_x.at[step, 1]),
@@ -192,7 +222,7 @@
     send_y[0, 0] = packed[0]
     send_y[0, 1] = packed[1]
     pl.semaphore_wait(barrier, len(neighbours))
-    started = [send(0, 0)]
+    started = [send(0, field.at[0])]
     for load in loads[2:]:
         load.wait()
 
@@ -205,11 +235,13 @@
         return carry
 
     lax.fori_loop(0, steps * planes, prepare, 0, unroll=4)
-
-    stores = []
+    macro_out[...] = macro[0]
+
+    buffers = [field.at[step % 2] for step in range(steps - 1)] + [field_out]
+
     for step in range(steps):
         saved = steps - 1 - step
-        source, target = step % 2, (step + 1) % 2
+        source = buffers[step]
         for copy in started[step]:
             copy.wait_recv()
         for corner, number in enumerate(CORNERS):
@@ -217,66 +249,66 @@
             end = ends[0] if SPEEDS[number][1] == 1 else ends[1]
             k = X_LISTS[side].index(number)
             recv_x[step, side, k] = jnp.where(end, recv_c[step, corner], recv_x[step, side, k])
-        last = step == steps - 1
+        if step == steps - 1:
+            halo_x_out[...] = recv_x[step]
+            halo_y_out[...] = recv_y[step]
+            break
+        target = buffers[step + 1]
+        halo_x = recv_x.at[step]
 
         def plane(z, carry):
             got, packed = carry
-            pulled = []
-            for number in range(COUNT):
-                cx, cy, cz = SPEEDS[number]
-                zz = lax.rem(z + (cz + planes), planes) if cz else z
-                value = field[source, number, zz]
-                if cy:
-                    side = 0 if cy == 1 else 1
-                    at = (SLOT * cz) % lanes + Y_LISTS[side].index(number)
-                    to = 0 if cy == 1 else lanes - 1
-                    column = pltpu.roll(got[side], (to - at) % lanes, 1)
-                    value = jnp.where(ends[side], column, value)
-                if cx:
-                    side = 0 if cx == 1 else 1
-                    k = X_LISTS[side].index(number)
-                    value = pltpu.roll(value, rows - 1 if cx == 1 else 1, 0)
-                    halo = jnp.broadcast_to(recv_x[step, side, k, pl.ds(zz, 1), :], (rows, lanes))
-                    value = jnp.where(edges[side], halo, value)
-                if cy:
-                    value = pltpu.roll(value, lanes - 1 if cy == 1 else 1, 1)
-                pulled.append(value)
+            pulled = pull_plane(z, source, halo_x, got, ends, edges)
             ux, uy, uz, cr = [macro[saved, k, z] for k in range(4)]
             f_out, h_out = transpose_collision(
                 pulled[:flow], pulled[flow:], ux, uy, uz, cr, lab[z]
             )
             values = f_out + h_out
             for number in range(COUNT):
-                field[target, number, z] = values[number]
-            if last:
-                return got, packed
+                target[number, z] = values[number]
             got = tuple(pltpu.roll(value, lanes - SLOT, 1) for value in got)
             return got, insert(packed, values)
 
-        def last_plane(z, carry):
-            carry = plane(z, carry)
-            got, packed = carry
-            got = tuple(pltpu.roll(value, lanes - SLOT, 1) for value in got)
-            return got, packed
-
         got = (recv_y[step, 0], recv_y[step, 1])
-        got, packed = lax.fori_loop(0, planes, last_plane if last else plane, (got, empty), unroll=8)
-        if not last:
-            send_y[step + 1, 0] = packed[0]
-            send_y[step + 1, 1] = packed[1]
-            started.append(send(step + 1, target))
-    final = steps % 2
-    stores = [
-        pltpu.make_async_copy(field.at[final, pl.ds(0, flow)], of_hbm, out_sem.at[0]),
-        pltpu.make_async_copy(field.at[final, pl.ds(flow, COUNT - flow)], ot_hbm, out_sem.at[1]),
-    ]
-    for store in stores:
-        store.start()
+        got, packed = lax.fori_loop(0, planes, plane, (got, empty), unroll=8)
+        send_y[step + 1, 0] = packed[0]
+        send_y[step + 1, 1] = packed[1]
+        started.append(send(step + 1, target))
     for copies in started:
         for copy in copies:
             copy.wait_send()
-    for store in stores:
-        store.wait()
+
+
+def finish(field, macro, halo_x, halo_y, lab, of_hbm, ot_hbm, stage, out_sem):
+    planes, rows, lanes = field.shape[1:]
+    flow = of_hbm.shape[0]
+    _, ends, edges = tiles(rows, lanes)
+
+    def stores(z):
+        return [
+            pltpu.make_async_copy(
+                stage.at[pl.ds(0, flow), z], of_hbm.at[:, z], out_sem.at[0, z]
+            ),
+            pltpu.make_async_copy(
+                stage.at[pl.ds(flow, COUNT - flow), z], ot_hbm.at[:, z], out_sem.at[1, z]
+            ),
+        ]
+
+    got = (halo_y[0], halo_y[1])
+    for z in range(planes):
+        pulled = pull_plane(z, field, halo_x, got, ends, edges)
+        ux, uy, uz, cr = [macro[k, z] for k in range(4)]
+        f_out, h_out = transpose_collision(
+            pulled[:flow], pulled[flow:], ux, uy, uz, cr, lab[z]
+        )
+        for number, value in enumerate(f_out + h_out):
+            stage[number, z] = value
+        for store in stores(z):
+            store.start()
+        got = tuple(pltpu.roll(value, lanes - SLOT, 1) for value in got)
+    for z in range(planes):
+        for store in stores(z):
+            store.wait()
 
 
 def body(saved_fluid, saved_tracer, adjoint_fluid, adjoint_tracer, label):
@@ -284,19 +316,23 @@
     tracer = saved_tracer.shape[1]
     f32 = jnp.float32
     tile = (rows, lanes)
-    return pl.pallas_call(
+    whole = (flow + tracer, planes) + tile
+    vmem, hbm = pl.BlockSpec(memory_space=pltpu.VMEM), pl.BlockSpec(memory_space=IN_SPACE)
+    ready = pl.pallas_call(
         kernel,
         out_shape=(
-            jax.ShapeDtypeStruct(adjoint_fluid.shape, f32),
-            jax.ShapeDtypeStruct(adjoint_tracer.shape, f32),
+            jax.ShapeDtypeStruct(whole, f32),
+            jax.ShapeDtypeStruct((4, planes) + tile, f32),
+            jax.ShapeDtypeStruct((2, 6, planes, lanes), f32),
+            jax.ShapeDtypeStruct((2,) + tile, f32),
+            jax.ShapeDtypeStruct(label.shape, label.dtype),
         ),
-        in_specs=[pl.BlockSpec(memory_space=pl.ANY)] * 5,
-        out_specs=[pl.BlockSpec(memory_space=pl.ANY)] * 2,
+        in_specs=[hbm] * 5,
+        out_specs=[vmem] * 5,
         scratch_shapes=[
             pltpu.VMEM(saved_fluid.shape, saved_fluid.dtype),
             pltpu.VMEM(saved_tracer.shape, saved_tracer.dtype),
-            pltpu.VMEM(label.shape, label.dtype),
-            pltpu.VMEM((2, flow + tracer, planes) + tile, f32),
+            pltpu.VMEM((2,) + whole, f32),
             pltpu.VMEM((steps, 4, planes) + tile, f32),
             pltpu.VMEM((steps, 2, 6, planes, lanes), f32),
             pltpu.VMEM((steps, 2, 6, planes, lanes), f32),
@@ -304,15 +340,29 @@
             pltpu.VMEM((steps, 2) + tile, f32),
             pltpu.VMEM((steps, 4, planes, lanes), f32),
             pltpu.SemaphoreType.DMA((5,)),
-            pltpu.SemaphoreType.DMA((2,)),
             pltpu.SemaphoreType.DMA((steps, 8)),
             pltpu.SemaphoreType.DMA((steps, 8)),
         ],
         compiler_params=pltpu.CompilerParams(
-            collective_id=0, has_side_effects=True, vmem_limit_bytes=60 * 1024 * 1024
+            collective_id=0, has_side_effects=True, vmem_limit_bytes=FIRST_VMEM
         ),
         name="adjoint_steps",
-    )(saved_fluid, saved_tracer, adjoint_fluid, adjoint_tracer, label)
+    )(*[pltpu.with_memory_space_constraint(value, pltpu.HBM) for value in (saved_fluid, saved_tracer, adjoint_fluid, adjoint_tracer, label)])
+    return pl.pallas_call(
+        finish,
+        out_shape=(
+            jax.ShapeDtypeStruct(adjoint_fluid.shape, f32),
+            jax.ShapeDtypeStruct(adjoint_tracer.shape, f32),
+        ),
+        in_specs=[vmem] * 5,
+        out_specs=[pl.BlockSpec(memory_space=pl.ANY)] * 2,
+        scratch_shapes=[
+            pltpu.VMEM(whole, f32),
+            pltpu.SemaphoreType.DMA((2, planes)),
+        ],
+        compiler_params=pltpu.CompilerParams(vmem_limit_bytes=16 * 1024 * 1024),
+        name="last_step",
+    )(*ready)
 
 
 def solution(mesh):

time: 25.4 us -> 22.6 us (0.89)
  local copies, waits for them, and re-layouts: 2.69 us -> 0 us
    unnamed x4 -> x0, local copies, waits for them, and re-layouts: 2.69 us -> none
    pallas_call x1 -> x2, Pallas kernels: 21.9 us -> 21.8 us  [the longest x1 20 us: body(): pl.pallas_call(kernel, out_shape=(jax.ShapeDtypeStruct(whole, f32), jax.S...]
where the time goes in v3:
time: 22.6 us; the launch traced here: 22.5 us
  Pallas kernels  21.8 us (96%)
  between operations  0.64 us (3%)
    pallas_call x1, Pallas kernels, body(): pl.pallas_call(kernel, out_shape=(jax.ShapeDtypeStruct(whole, f32), jax.S...  20 us
    pallas_call x1, Pallas kernels, body(): pl.pallas_call(finish, out_shape=(jax.ShapeDtypeStruct(adjoint_fluid.shap...  1.82 us

profile of v3, /device:TPU:0, one launch (start us, length us, event | category | flops | bytes accessed | tf_op | source)
XLA Modules:
  0.0 22.5 jit_solution(6351505781895004488)
XLA Ops:
  0.6 20.0 %adjoint_steps.1 = (f32[26,8,8,128]{3,2,1,0:T(8,128)S(1)}, f32[4,8,8,128]{3,2,1,0:T(8,128)S(1)}, f32[2,6,8,128]{3,2,1,0:T(8,128)S(1)}, f32[2,8,128]{2,1,0:T(8,128)S(1)}, s32[8,8,128]{2,1,0:T(8,128)S(1)}) custom-call(bf16[3,19,8,8,128]{4,3,2,1,0:T(8,128)(2,1)} %sf_hbm.1, bf16[3,7,8,8,128]{4,3,2,1,0:T(8,128)(2,1)} %st_hbm.1, f32[19,8,8,128]{3,2,1,0:T(8,128)} %af_hbm.1, ...), custom_call_target="tpu_custom_call" | custom-call | tf_op jit(solution)/shard_map/adjoint_steps/pallas_call | solution.py:321
  20.7 1.8 %last_step.1 = (f32[19,8,8,128]{3,2,1,0:T(8,128)}, f32[7,8,8,128]{3,2,1,0:T(8,128)}) custom-call(f32[26,8,8,128]{3,2,1,0:T(8,128)S(1)} %get-tuple-element.7.field, f32[4,8,8,128]{3,2,1,0:T(8,128)S(1)} %get-tuple-element.8.macro, f32[2,6,8,128]{3,2,1,0:T(8,128)S(1)} %get-tuple-element.9.halo_x, f32[2,8,128]{2,1,0:T(8,128)S(1)} %get-tuple-element.10.halo_y, ...), custom_call_target="tpu_custom_call" | custom-call | tf_op jit(solution)/shard_map/last_step/pallas_call | solution.py:351

commit v4 on v3

--- a/solution.py
+++ b/solution.py
@@ -111,6 +111,14 @@
     return lane, [lane == 0, lane == lanes - 1], [row == rows - 1, row == 0]
 
 
+def turn(value, cx, cy, rows, lanes):
+    if cx:
+        value = pltpu.roll(value, rows - 1 if cx == 1 else 1, 0)
+    if cy:
+        value = pltpu.roll(value, lanes - 1 if cy == 1 else 1, 1)
+    return value
+
+
 def pull_plane(z, field, halo_x, got, ends, edges):
     planes, rows, lanes = field.shape[1:]
     pulled = []
@@ -121,17 +129,14 @@
         if cy:
             side = 0 if cy == 1 else 1
             at = (SLOT * cz) % lanes + Y_LISTS[side].index(number)
-            to = 0 if cy == 1 else lanes - 1
-            column = pltpu.roll(got[side], (to - at) % lanes, 1)
-            value = jnp.where(ends[side], column, value)
+            to = lanes - 1 if cy == 1 else 0
+            column = turn(pltpu.roll(got[side], (to - at) % lanes, 1), cx, 0, rows, lanes)
+            value = jnp.where(ends[1 - side], column, value)
         if cx:
             side = 0 if cx == 1 else 1
             k = X_LISTS[side].index(number)
-            value = pltpu.roll(value, rows - 1 if cx == 1 else 1, 0)
             halo = jnp.broadcast_to(halo_x[side, k, pl.ds(zz, 1), :], (rows, lanes))
             value = jnp.where(edges[side], halo, value)
-        if cy:
-            value = pltpu.roll(value, lanes - 1 if cy == 1 else 1, 1)
         pulled.append(value)
     return pulled
 
@@ -154,7 +159,7 @@
         (x_prior, y_prior), (x_next, y_next), (x_prior, y_next), (x_next, y_prior),
     ]
     barrier = pltpu.get_barrier_semaphore()
-    for device in neighbours:
+    for device in neighbours[4:] + neighbours[:4]:
         pl.semaphore_signal(barrier, inc=1, device_id=device, device_id_type=MESH)
 
     loads = [
@@ -164,7 +169,7 @@
         pltpu.make_async_copy(st_hbm, st, in_sem.at[3]),
         pltpu.make_async_copy(lab_hbm, lab, in_sem.at[4]),
     ]
-    for load in loads:
+    for load in loads[:2]:
         load.start()
 
     lane, ends, edges = tiles(rows, lanes)
@@ -180,10 +185,12 @@
         return tuple(done)
 
     def send(step, source):
-        for side in range(2):
-            at = 0 if side == 0 else rows - 1
-            for k, number in enumerate(X_LISTS[side]):
-                send_x[step, side, k] = source[number, :, at, :]
+        def face(slots):
+            for side in range(2):
+                at = 0 if side == 0 else rows - 1
+                for k in slots:
+                    send_x[step, side, k] = source[X_LISTS[side][k], :, at, :]
+
         pairs = [
             (send_x.at[step, 0], recv_x.at[step, 0]),
             (send_x.at[step, 1], recv_x.at[step, 1]),
@@ -194,24 +201,29 @@
             (send_x.at[step, 0, 2], recv_c.at[step, 2]),
             (send_x.at[step, 1, 2], recv_c.at[step, 3]),
         ]
-        copies = []
-        for number, ((source_ref, target_ref), device) in enumerate(zip(pairs, neighbours)):
-            copies.append(
-                pltpu.make_async_remote_copy(
-                    src_ref=source_ref,
-                    dst_ref=target_ref,
-                    send_sem=send_sem.at[step, number],
-                    recv_sem=recv_sem.at[step, number],
-                    device_id=device,
-                    device_id_type=MESH,
-                )
+        copies = [
+            pltpu.make_async_remote_copy(
+                src_ref=source_ref,
+                dst_ref=target_ref,
+                send_sem=send_sem.at[step, number],
+                recv_sem=recv_sem.at[step, number],
+                device_id=device,
+                device_id_type=MESH,
             )
-        for copy in copies:
+            for number, ((source_ref, target_ref), device) in enumerate(zip(pairs, neighbours))
+        ]
+        face((1, 2))
+        for copy in copies[4:] + copies[2:4]:
+            copy.start()
+        face((0, 3, 4, 5))
+        for copy in copies[:2]:
             copy.start()
         return copies
 
     loads[0].wait()
     loads[1].wait()
+    for load in loads[2:]:
+        load.start()
 
     def first_pack(z, packed):
         values = {n: field[0, n, z] for side in Y_LISTS for n in side}
@@ -242,13 +254,23 @@
     for step in range(steps):
         saved = steps - 1 - step
         source = buffers[step]
+
+        def turn_plane(z, carry):
+            for number in range(COUNT):
+                cx, cy, _ = SPEEDS[number]
+                if cx or cy:
+                    source[number, z] = turn(source[number, z], cx, cy, rows, lanes)
+            return carry
+
+        lax.fori_loop(0, planes, turn_plane, 0, unroll=2)
         for copy in started[step]:
             copy.wait_recv()
         for corner, number in enumerate(CORNERS):
             side = 0 if SPEEDS[number][0] == 1 else 1
             end = ends[0] if SPEEDS[number][1] == 1 else ends[1]
             k = X_LISTS[side].index(number)
-            recv_x[step, side, k] = jnp.where(end, recv_c[step, corner], recv_x[step, side, k])
+            merged = jnp.where(end, recv_c[step, corner], recv_x[step, side, k])
+            recv_x[step, side, k] = turn(merged, 0, SPEEDS[number][1], rows, lanes)
         if step == steps - 1:
             halo_x_out[...] = recv_x[step]
             halo_y_out[...] = recv_y[step]

time: 22.6 us -> 22 us (0.973)
  Pallas kernels: 21.8 us -> 21.2 us
    pallas_call x1, Pallas kernels: 20 us -> 19.6 us  [body(): pl.pallas_call(kernel, out_shape=(jax.ShapeDtypeStruct(whole, f32), jax.S...]
where the time goes in v4:
time: 22 us; the launch traced here: 21.8 us
  Pallas kernels  21.2 us (96%)
  between operations  0.64 us (3%)
    pallas_call x1, Pallas kernels, body(): pl.pallas_call(kernel, out_shape=(jax.ShapeDtypeStruct(whole, f32), jax.S...  19.6 us
    pallas_call x1, Pallas kernels, body(): pl.pallas_call(finish, out_shape=(jax.ShapeDtypeStruct(adjoint_fluid.shap...  1.6 us

profile of v4, /device:TPU:0, one launch (start us, length us, event | category | flops | bytes accessed | tf_op | source)
XLA Modules:
  0.0 21.8 jit_solution(14670846760104616765)
XLA Ops:
  0.6 19.6 %adjoint_steps.1 = (f32[26,8,8,128]{3,2,1,0:T(8,128)S(1)}, f32[4,8,8,128]{3,2,1,0:T(8,128)S(1)}, f32[2,6,8,128]{3,2,1,0:T(8,128)S(1)}, f32[2,8,128]{2,1,0:T(8,128)S(1)}, s32[8,8,128]{2,1,0:T(8,128)S(1)}) custom-call(bf16[3,19,8,8,128]{4,3,2,1,0:T(8,128)(2,1)} %sf_hbm.1, bf16[3,7,8,8,128]{4,3,2,1,0:T(8,128)(2,1)} %st_hbm.1, f32[19,8,8,128]{3,2,1,0:T(8,128)} %af_hbm.1, ...), custom_call_target="tpu_custom_call" | custom-call | tf_op jit(solution)/shard_map/adjoint_steps/pallas_call | solution.py:343
  20.2 1.6 %last_step.1 = (f32[19,8,8,128]{3,2,1,0:T(8,128)}, f32[7,8,8,128]{3,2,1,0:T(8,128)}) custom-call(f32[26,8,8,128]{3,2,1,0:T(8,128)S(1)} %get-tuple-element.7.field, f32[4,8,8,128]{3,2,1,0:T(8,128)S(1)} %get-tuple-element.8.macro, f32[2,6,8,128]{3,2,1,0:T(8,128)S(1)} %get-tuple-element.9.halo_x, f32[2,8,128]{2,1,0:T(8,128)S(1)} %get-tuple-element.10.halo_y, ...), custom_call_target="tpu_custom_call" | custom-call | tf_op jit(solution)/shard_map/last_step/pallas_call | solution.py:373

commit v5 on v4

--- a/solution.py
+++ b/solution.py
@@ -235,19 +235,15 @@
     send_y[0, 1] = packed[1]
     pl.semaphore_wait(barrier, len(neighbours))
     started = [send(0, field.at[0])]
-    for load in loads[2:]:
-        load.wait()
-
-    def prepare(index, carry):
-        step, z = index // planes, index % planes
-        f = [sf[step, n, z].astype(jnp.float32) for n in range(flow)]
-        h = [st[step, n, z].astype(jnp.float32) for n in range(COUNT - flow)]
-        for k, value in enumerate(macros(f, h)):
-            macro[step, k, z] = value
-        return carry
-
-    lax.fori_loop(0, steps * planes, prepare, 0, unroll=4)
-    macro_out[...] = macro[0]
+    def prepare_step(step, into):
+        def prepare(z, carry):
+            f = [sf[step, n, z].astype(jnp.float32) for n in range(flow)]
+            h = [st[step, n, z].astype(jnp.float32) for n in range(COUNT - flow)]
+            for k, value in enumerate(macros(f, h)):
+                into[k, z] = value
+            return carry
+
+        lax.fori_loop(0, planes, prepare, 0, unroll=4)
 
     buffers = [field.at[step % 2] for step in range(steps - 1)] + [field_out]
 
@@ -263,6 +259,10 @@
             return carry
 
         lax.fori_loop(0, planes, turn_plane, 0, unroll=2)
+        if step == 0:
+            for load in loads[2:]:
+                load.wait()
+        prepare_step(saved, macro_out if saved == 0 else macro.at[saved])
         for copy in started[step]:
             copy.wait_recv()
         for corner, number in enumerate(CORNERS):

time: 22 us -> 22 us (level)
  no operation moved by 1% of the time
where the time goes in v5:
time: 22 us; the launch traced here: 21.8 us
  Pallas kernels  21.2 us (96%)
  between operations  0.64 us (3%)
    pallas_call x1, Pallas kernels, body(): pl.pallas_call(kernel, out_shape=(jax.ShapeDtypeStruct(whole, f32), jax.S...  19.6 us
    pallas_call x1, Pallas kernels, body(): pl.pallas_call(finish, out_shape=(jax.ShapeDtypeStruct(adjoint_fluid.shap...  1.6 us

profile of v5, /device:TPU:0, one launch (start us, length us, event | category | flops | bytes accessed | tf_op | source)
XLA Modules:
  0.0 21.8 jit_solution(5400304785605605319)
XLA Ops:
  0.6 19.6 %adjoint_steps.1 = (f32[26,8,8,128]{3,2,1,0:T(8,128)S(1)}, f32[4,8,8,128]{3,2,1,0:T(8,128)S(1)}, f32[2,6,8,128]{3,2,1,0:T(8,128)S(1)}, f32[2,8,128]{2,1,0:T(8,128)S(1)}, s32[8,8,128]{2,1,0:T(8,128)S(1)}) custom-call(bf16[3,19,8,8,128]{4,3,2,1,0:T(8,128)(2,1)} %sf_hbm.1, bf16[3,7,8,8,128]{4,3,2,1,0:T(8,128)(2,1)} %st_hbm.1, f32[19,8,8,128]{3,2,1,0:T(8,128)} %af_hbm.1, ...), custom_call_target="tpu_custom_call" | custom-call | tf_op jit(solution)/shard_map/adjoint_steps/pallas_call | solution.py:343
  20.2 1.6 %last_step.1 = (f32[19,8,8,128]{3,2,1,0:T(8,128)}, f32[7,8,8,128]{3,2,1,0:T(8,128)}) custom-call(f32[26,8,8,128]{3,2,1,0:T(8,128)S(1)} %get-tuple-element.7.field, f32[4,8,8,128]{3,2,1,0:T(8,128)S(1)} %get-tuple-element.8.macro, f32[2,6,8,128]{3,2,1,0:T(8,128)S(1)} %get-tuple-element.9.halo_x, f32[2,8,128]{2,1,0:T(8,128)S(1)} %get-tuple-element.10.halo_y, ...), custom_call_target="tpu_custom_call" | custom-call | tf_op jit(solution)/shard_map/last_step/pallas_call | solution.py:373
